TPU v7x, 32 devices: a whole 2x2x4 slice. The times are simulated.
32 devices in a mesh: chan: 16 (over z, x, core), day: 2 (over y).
Axes of the slice: x: 2, y: 2, z: 4, core: 2. Of those that a mesh axis runs over, the one named last changes fastest.
Arguments:
- spectra: bfloat16 [2, 256, 2, 4096], P('day', 'chan'), may hold values from -6 to 6
- source_index: int32 [16], replicated, may hold values from 0 to 255, as said below
- interrogator: int32 [256], P('chan'), may hold values from 0 to 7, as said below
- lag_bounds: int32 [16, 2], replicated, may hold values from 0 to 256, as said below
Outputs:
- reference_stack: bfloat16 [16, 256, 256], P('day', 'chan')
- drift: float32 [2, 8], P('day')
Inputs may be any that keep to these rules, and one draw needn't show every extreme that they name: `source_index`: distinct channels. Each interrogator serves one contiguous run of channels, in rising order, of at least 16 channels. `lag_bounds`: first lag below end lag, and each window spans at least 128 lags.
All inputs are finite; a program needn't handle non-finite values.
Results may differ from a plain program's by a relative error of at most 0.0065.
Values may be sent and summed in bfloat16 or wider, within the bound.
A program may use at most 64 MiB of HBM per device.

v0:
```python
import math

import jax
import jax.numpy as jnp
from jax import lax
from jax.sharding import PartitionSpec as P

LAGS = 256
NINT = 8


def lag_table(bins, lags):
    freq = jnp.arange(bins, dtype=jnp.int32)
    shift = jnp.arange(lags, dtype=jnp.int32) - lags // 2
    phase = freq[:, None] * shift[None, :] % (2 * bins)
    angle = math.pi * phase.astype(jnp.float32) / bins
    scale = 1.0 / math.sqrt(bins)
    return jnp.concatenate([jnp.cos(angle) * scale, -jnp.sin(angle) * scale], 0).astype(
        jnp.bfloat16
    )


def per_device(spectra, source_index, interrogator, lag_bounds):
    day_dev, ch_dev, _, bins = spectra.shape
    nsrc = source_index.shape[0]
    lags = LAGS
    offset = lax.axis_index("chan") * ch_dev
    chan_ids = offset + jnp.arange(ch_dev, dtype=jnp.int32)
    select = (source_index[:, None] == chan_ids[None, :]).astype(jnp.bfloat16)
    flat = spectra.reshape(day_dev, ch_dev, 2 * bins)
    picked = jnp.einsum("sc,dcf->dsf", select, flat, preferred_element_type=jnp.float32)
    summed = lax.psum(picked.astype(jnp.bfloat16), "chan")
    sources = summed.reshape(day_dev, nsrc, 2, bins)
    table = lag_table(bins, lags)
    block = math.gcd(nsrc, 16)

    def correlate_block(index, corr):
        chosen = sources[0].astype(jnp.float32)
        local = spectra[0].astype(jnp.float32)
        real_in = local[None, :, 0]
        imag_in = local[None, :, 1]
        real_src = chosen[:, None, 0]
        imag_src = chosen[:, None, 1]
        cross = jnp.concatenate(
            [real_in * real_src + imag_in * imag_src, imag_in * real_src - real_in * imag_src], -1
        )
        cross = cross.astype(jnp.bfloat16).reshape(block * ch_dev, 2 * bins)
        result = jnp.dot(cross, table, preferred_element_type=jnp.float32).reshape(
            1, block, ch_dev, lags
        )
        return result

    corr = lax.fori_loop(
        0, nsrc // block, correlate_block, jnp.zeros((day_dev, nsrc, ch_dev, lags), jnp.float32)
    )
    local_sum = jnp.sum(corr, 0)
    days = day_dev * lax.axis_size("day")
    total = lax.psum(local_sum, "day")
    ref_full = (total / days).astype(jnp.bfloat16)
    share = nsrc // lax.axis_size("day")
    ref_out = lax.dynamic_slice_in_dim(ref_full, lax.axis_index("day") * share, share, 0)
    ref_float = ref_full.astype(jnp.float32)
    lag_pos = jnp.arange(lags, dtype=jnp.int32)
    window = (
        (lag_pos[None, :] >= lag_bounds[:, 0:1]) & (lag_pos[None, :] < lag_bounds[:, 1:2])
    ).astype(jnp.float32)
    member = (interrogator[:, None] == jnp.arange(NINT, dtype=jnp.int32)[None, :]).astype(
        jnp.float32
    )
    day_corr = corr[0]
    padded = jnp.pad(day_corr, ((0, 0), (0, 0), (1, 1)))
    slope = 0.5 * (padded[:, :, 2:] - padded[:, :, :-2])
    weighted = window[:, None, :] * slope
    num_chan = jnp.sum(weighted * (day_corr - ref_float), axis=(0, 2))
    den_chan = jnp.sum(weighted * slope, axis=(0, 2))
    numers = [jnp.sum(num_chan[:, None] * member, 0)]
    denoms = [jnp.sum(den_chan[:, None] * member, 0)]
    numer, denom = lax.psum((jnp.stack(numers, 0), jnp.stack(denoms, 0)), "chan")
    drift = numer / (denom + 1e-06)
    return (ref_out, drift)


def solution(mesh):
    return jax.shard_map(
        per_device,
        mesh=mesh,
        in_specs=(P("day", "chan", None, None), P(), P("chan"), P()),
        out_specs=(P("day", "chan", None), P("day", None)),
        check_vma=False,
    )
```

profile of v0, /device:TPU:0, one launch (start us, length us, event | category | flops | bytes accessed | tf_op | source)
XLA Modules:
  0.0 175.2 jit_solution(15866819684879410157)
XLA Ops:
  7.2 0.0 all-reduce.5.cloned.1.call-start
  7.2 1.1 copy.10
  8.3 0.9 fusion
  9.3 0.9 convert_element_type.56
  10.2 0.0 all-reduce.5.cloned.1.call-update
  10.2 0.0 all-reduce.7.cloned.1.call-start
  10.2 1.2 bitcast_convert_fusion
  11.4 0.6 fusion.21
  12.0 18.2 %multiply_convert_fusion.1 = (bf16[4096,256]{1,0:T(8,128)(2,1)S(1)}, bf16[4096,256]{1,0:T(8,128)(2,1)}) fusion(s32[256]{0:T(256)S(1)} %iota_add_fusion), kind=kLoop, calls=%fused_computation.16 | loop fusion | flops 19922944 | bytes 4195328 | tf_op jit(solution)/shard_map/convert.2
  30.2 0.3 copy_bitcast_fusion.1
  30.5 72.4 %all-reduce.5.cloned.1.call-done = bf16[16,2,4096]{2,1,0:T(2,128)(2,1)} async-done(((bf16[16,2,4096]{2,1,0:T(2,128)(2,1)}), bf16[16,2,4096]{2,1,0:T(2,128)(2,1)}) %all-reduce.5.cloned.1.call-update) | async-done | bytes 262160 | tf_op jit(solution)/shard_map/psum | solution.py:32
  102.9 1.6 fusion.22
  104.5 0.3 copy_bitcast_fusion
  104.8 0.0 copy-start
  104.8 1.1 add_convert_fusion
  105.9 0.5 copy-done
  106.4 0.0 copy-start.1
  106.4 0.0 copy-start.2
  106.4 2.0 %fusion.4 = f32[256,256]{1,0:T(8,128)} fusion(bf16[256,4096]{1,0:T(8,128)(2,1)S(1)} %bitcast.31, bf16[256,4096]{1,0:T(8,128)(2,1)S(1)} %bitcast.30, bf16[4096,256]{1,0:T(8,128)(2,1)S(1)} %copy-done, bf16[4096,256]{1,0:T(8,128)(2,1)S(1)} %get-tuple-element.29), kind=kOutput, calls=%fused_computation.8 | convolution fusion | flops 1090519040 | bytes 8650752 | tf_op jit(solution)/shard_map/while/body/eval_jaxpr/dot_general | solution.py:48
  108.4 0.0 all-reduce.7.cloned.1.call-update
  108.4 0.0 copy-done.1
  108.4 0.1 fusion.16
  108.5 23.8 %all-reduce.7.cloned.1.call-done = f32[16,16,256]{2,1,0:T(8,128)} async-done(((f32[16,16,256]{2,1,0:T(8,128)}), f32[16,16,256]{2,1,0:T(8,128)}) %all-reduce.7.cloned.1.call-update) | async-done | bytes 262160 | tf_op jit(solution)/shard_map/psum | solution.py:58
  132.3 2.1 %multiply_reduce_fusion = (f32[16]{0:T(128)S(1)}, f32[16]{0:T(128)S(1)}, bf16[16,16,256]{2,1,0:T(8,128)(2,1)S(1)}) fusion(f32[16,256]{1,0:T(8,128)S(1)} %fusion.16, f32[16,16,256]{2,1,0:T(8,128)} %bitcast.34, f32[16,16,256]{2,1,0:T(8,128)} %all-reduce.7.cloned.1.call-done), kind=kLoop, calls=%fused_computation.30 | loop fusion | flops 851936 | bytes 671872 | tf_op jit(solution)/shard_map/reduce_sum | solution.py:75
  134.3 0.0 copy-done.2
  134.3 0.1 select_reduce_fusion
  134.5 32.7 %all-reduce.1 = (f32[1,8]{1,0:T(1,128)S(1)}, f32[1,8]{1,0:T(1,128)S(1)}) all-reduce(f32[1,8]{1,0:T(1,128)S(1)} %bitcast.37, f32[1,8]{1,0:T(1,128)S(1)} %bitcast.36), channel_id=1, replica_groups=mesh['chan'=16,'day'=2] {'chan'}, use_global_device_ids=true, to_apply=%region_4.5 | all-reduce | flops 16 | bytes 128 | tf_op jit(solution)/shard_map/psum | solution.py:78
  167.2 0.5 add_divide_fusion
  167.7 0.6 constant_dynamic-slice_fusion
  (3 shorter events, 0.0 us)
Async XLA Ops:
  7.2 95.7 %all-reduce.5.cloned.1.call-start = ((), (), s32[]{:S(2)}) async-start(), calls=%async_computation | async-start | bytes 524288 | tf_op jit(solution)/shard_map/psum | solution.py:32
  10.2 122.1 %all-reduce.7.cloned.1.call-start = ((), (), s32[]{:S(2)}) async-start(), calls=%async_computation.1 | async-start | bytes 524288 | tf_op jit(solution)/shard_map/psum | solution.py:58
  104.8 1.6 copy-start
  106.4 2.0 %copy-start.1 = (s32[16,2]{0,1:T(2,128)S(1)}, s32[16,2]{0,1:T(2,128)}, u32[]{:S(2)}) copy-start(s32[16,2]{0,1:T(2,128)} %param.7) | copy-start | bytes 388
  106.4 27.9 %copy-start.2 = (s32[16]{0:T(128)S(1)}, s32[16]{0:T(128)}, u32[]{:S(2)}) copy-start(s32[16]{0:T(128)} %param.6) | copy-start | bytes 196
Sparse Core Ops, SparseCore 0:
  11.4 91.4 all-reduce.4
  108.5 23.7 all-reduce.6
where the time goes:
time: 175 us
  waiting for transfers between devices  96.2 us (55%)
  blocking collectives  32.7 us (19%)
  other arithmetic  23.3 us (13%)
  between operations  14.1 us (8%)
  local copies, waits for them, and re-layouts  5.83 us (3%)
  matrix products  2.9 us (2%)
    psum x1, waiting for transfers between devices, per_device(): summed = lax.psum(picked.astype(jnp.bfloat16), 'chan')  72.4 us
    psum x1, blocking collectives, per_device(): lax.psum((jnp.stack(numers, 0), jnp.stack(denoms, 0)), 'chan')  32.7 us
    psum x1, waiting for transfers between devices, per_device(): total = lax.psum(local_sum, 'day')  23.8 us
    another operation x2, other arithmetic  19.4 us
  transfers between devices with their start and end apart: 2, of which 2 were waited for; matrix products, arithmetic and copies ran while one was open for 12% of the time, Pallas kernels for 0%

commit v1 on v0

v1 whole, which is shorter than its diff:
```python
import functools
import math

import jax
import jax.numpy as jnp
import numpy as np
from jax import lax
from jax.experimental import pallas as pl
from jax.experimental.pallas import tpu as pltpu
from jax.sharding import PartitionSpec as P

LAGS = 256
NINT = 8
LANES = 128
MESH = pl.DeviceIdType.MESH


def lag_table(bins, lags):
    freq = np.arange(bins, dtype=np.int32)
    shift = np.arange(lags, dtype=np.int32) - lags // 2
    phase = freq[:, None] * shift[None, :] % (2 * bins)
    angle = np.float32(math.pi) * phase.astype(np.float32) / np.float32(bins)
    scale = np.float32(1.0 / math.sqrt(bins))
    return np.stack([np.cos(angle) * scale, -np.sin(angle) * scale]).astype(jnp.bfloat16)


def column(row):
    m = row.shape[1]
    wide = jnp.broadcast_to(row.astype(jnp.float32), (m, m))
    eye = lax.broadcasted_iota(jnp.int32, (m, m), 0) == lax.broadcasted_iota(jnp.int32, (m, m), 1)
    return jnp.sum(jnp.where(eye, wide, 0.0), axis=1, keepdims=True)


def kernel(
    n, days, bounds_ref, index_ref, inter_ref, local_ref, table_hbm, ref_out, drift_out,
    table, mine, parts, gath, cross, acc, day_send, day_recv, fit,
    table_sem, rs_send, rs_recv, ag_send, ag_recv, dy_send, dy_recv, ft_send, ft_recv,
):
    me = lax.axis_index("chan")
    today = lax.axis_index("day")
    ch = local_ref.shape[2]
    nsrc = mine.shape[2]
    chunk = mine.shape[3]
    share = nsrc // days
    rows = share * ch

    load = pltpu.make_async_copy(table_hbm, table, table_sem)
    load.start()

    barrier = pltpu.get_barrier_semaphore()

    def greet(step, carry):
        c = lax.rem(me + lax.rem(step, n), n)
        d = lax.rem(today + step // n, days)
        pl.semaphore_signal(barrier, inc=1, device_id={"chan": c, "day": d}, device_id_type=MESH)
        return carry

    lax.fori_loop(1, n * days, greet, 0)

    wanted = column(index_ref[...]) - (me * ch).astype(jnp.float32)
    select = (
        wanted == lax.broadcasted_iota(jnp.int32, (nsrc, ch), 1).astype(jnp.float32)
    ).astype(jnp.bfloat16)

    def pick(j, carry):
        for part in range(2):
            mine[j, part] = jnp.dot(
                select, local_ref[j, part], preferred_element_type=jnp.float32
            ).astype(jnp.bfloat16)
        return carry

    lax.fori_loop(0, n, pick, 0)
    pl.semaphore_wait(barrier, n * days - 1)

    def scatter(k):
        peer = lax.rem(me + k, n)
        return pltpu.make_async_remote_copy(
            src_ref=mine.at[peer], dst_ref=parts.at[k], send_sem=rs_send.at[k],
            recv_sem=rs_recv.at[k], device_id={"chan": peer}, device_id_type=MESH,
        )

    def gather(k):
        peer = lax.rem(me + k, n)
        return pltpu.make_async_remote_copy(
            src_ref=gath.at[0], dst_ref=gath.at[k], send_sem=ag_send.at[k],
            recv_sem=ag_recv.at[k], device_id={"chan": peer}, device_id_type=MESH,
        )

    for k in range(1, n):
        scatter(k).start()
    own = mine[me].astype(jnp.float32)
    for k in range(1, n):
        scatter(k).wait_recv()
        own = own + parts[k].astype(jnp.float32)
    gath[0] = own.astype(jnp.bfloat16)
    for k in range(1, n):
        gather(k).start()
    load.wait()

    def correlate(k):
        j = lax.rem(me - k + n, n)
        sr = local_ref[j, 0].astype(jnp.float32)
        si = local_ref[j, 1].astype(jnp.float32)
        vr = gath[k, 0].astype(jnp.float32)
        vi = gath[k, 1].astype(jnp.float32)
        for s in range(nsrc):
            ar, ai = vr[s : s + 1], vi[s : s + 1]
            at = pl.ds(s * ch, ch)
            cross[at, :chunk] = (sr * ar + si * ai).astype(jnp.bfloat16)
            cross[at, chunk:] = (si * ar - sr * ai).astype(jnp.bfloat16)
        return jnp.dot(cross[...], table[j], preferred_element_type=jnp.float32)

    acc[...] = correlate(0)

    def step(k, carry):
        gather(k).wait_recv()
        acc[...] += correlate(k)
        return carry

    lax.fori_loop(1, n, step, 0)

    def exchange(k):
        peer = lax.rem(today + k, days)
        return pltpu.make_async_remote_copy(
            src_ref=day_send.at[peer], dst_ref=day_recv.at[k], send_sem=dy_send.at[k],
            recv_sem=dy_recv.at[k], device_id={"day": peer}, device_id_type=MESH,
        )

    for d in range(days):
        day_send[d] = acc[d * rows : (d + 1) * rows].astype(jnp.bfloat16)
    for k in range(1, days):
        exchange(k).start()

    def finish(kc, kd):
        at = kd * n + kc
        return pltpu.make_async_remote_copy(
            src_ref=fit.at[n * days + kd], dst_ref=fit.at[at], send_sem=ft_send.at[at],
            recv_sem=ft_recv.at[at],
            device_id={"chan": lax.rem(me + kc, n), "day": lax.rem(today - kd + days, days)},
            device_id_type=MESH,
        )

    lag = lax.broadcasted_iota(jnp.int32, (ch, LAGS), 1)
    member = (
        column(inter_ref[...]) == lax.broadcasted_iota(jnp.int32, (ch, LANES), 1).astype(jnp.float32)
    ).astype(jnp.float32)
    late = (
        column(inter_ref[...]) + LANES // 2
        == lax.broadcasted_iota(jnp.int32, (ch, LANES), 1).astype(jnp.float32)
    ).astype(jnp.float32)
    base = today * rows
    for k in range(1, days):
        exchange(k).wait_recv()
    nums = [jnp.zeros((ch, LAGS), jnp.float32) for _ in range(days)]
    dens = [jnp.zeros((ch, LAGS), jnp.float32) for _ in range(days)]
    for s in range(share):
        corrs = [acc[pl.ds(pl.multiple_of(base + s * ch, ch), ch)]]
        for k in range(1, days):
            corrs.append(day_recv[k, s * ch : (s + 1) * ch].astype(jnp.float32))
        mean = (sum(corrs[1:], corrs[0]) / days).astype(jnp.bfloat16)
        ref_out[s] = mean
        mean = mean.astype(jnp.float32)
        lo = bounds_ref[today * share + s, 0]
        hi = bounds_ref[today * share + s, 1]
        inside = (lag >= lo) & (lag < hi)
        for k in range(days):
            after = jnp.where(lag == LAGS - 1, 0.0, pltpu.roll(corrs[k], LAGS - 1, 1))
            before = jnp.where(lag == 0, 0.0, pltpu.roll(corrs[k], 1, 1))
            slope = 0.5 * (after - before)
            weighted = jnp.where(inside, slope, 0.0)
            nums[k] = nums[k] + weighted * (corrs[k] - mean)
            dens[k] = dens[k] + weighted * slope
    for k in range(days):
        num = jnp.sum(nums[k], axis=1, keepdims=True)
        den = jnp.sum(dens[k], axis=1, keepdims=True)
        fit[n * days + k] = jnp.sum(num * member + den * late, axis=0, keepdims=True)
    for kd in range(days):
        def send(kc, carry, kd=kd):
            finish(kc, kd).start()
            return carry

        lax.fori_loop(1 if kd == 0 else 0, n, send, 0)
    total = fit[n * days]

    def collect(at, total):
        finish(lax.rem(at, n), at // n).wait_recv()
        return total + fit[at]

    total = lax.fori_loop(1, n * days, collect, total)
    drift_out[...] = (total / (pltpu.roll(total, LANES // 2, 1) + 1e-06))[:, :NINT]

    for k in range(1, n):
        scatter(k).wait_send()
        gather(k).wait_send()
    for k in range(1, days):
        exchange(k).wait_send()

    def drain(at, carry):
        finish(lax.rem(at, n), at // n).wait_send()
        return carry

    lax.fori_loop(1, n * days, drain, 0)


def per_device(n, days, spectra, source_index, interrogator, lag_bounds):
    _, ch, _, bins = spectra.shape
    nsrc = source_index.shape[0]
    chunk = bins // n
    share = nsrc // days
    table = lag_table(bins, LAGS).reshape(2, n, chunk, LAGS).transpose(1, 0, 2, 3)
    table = jnp.asarray(table.reshape(n, 2 * chunk, LAGS))
    local = spectra[0].reshape(ch, 2, n, chunk).transpose(2, 1, 0, 3)
    vmem = pl.BlockSpec(memory_space=pltpu.VMEM)
    dma = pltpu.SemaphoreType.DMA
    bf16, f32 = jnp.bfloat16, jnp.float32
    ref_out, drift = pl.pallas_call(
        functools.partial(kernel, n, days),
        out_shape=(
            jax.ShapeDtypeStruct((share, ch, LAGS), bf16),
            jax.ShapeDtypeStruct((1, NINT), f32),
        ),
        in_specs=[
            pl.BlockSpec(memory_space=pltpu.SMEM), vmem, vmem, vmem,
            pl.BlockSpec(memory_space=pl.ANY),
        ],
        out_specs=(vmem, vmem),
        scratch_shapes=[
            pltpu.VMEM((n, 2 * chunk, LAGS), bf16),
            pltpu.VMEM((n, 2, nsrc, chunk), bf16),
            pltpu.VMEM((n, 2, nsrc, chunk), bf16),
            pltpu.VMEM((n, 2, nsrc, chunk), bf16),
            pltpu.VMEM((nsrc * ch, 2 * chunk), bf16),
            pltpu.VMEM((nsrc * ch, LAGS), f32),
            pltpu.VMEM((days, share * ch, LAGS), bf16),
            pltpu.VMEM((days, share * ch, LAGS), bf16),
            pltpu.VMEM((n * days + days, 1, LANES), f32),
            dma, dma((n,)), dma((n,)), dma((n,)), dma((n,)), dma((days,)), dma((days,)),
            dma((n * days,)), dma((n * days,)),
        ],
        compiler_params=pltpu.CompilerParams(
            collective_id=0, has_side_effects=True, vmem_limit_bytes=32 * 1024 * 1024
        ),
    )(lag_bounds, source_index[None], interrogator[None], local, table)
    return ref_out, drift


def solution(mesh):
    return jax.shard_map(
        functools.partial(per_device, mesh.shape["chan"], mesh.shape["day"]),
        mesh=mesh,
        in_specs=(P("day", "chan", None, None), P(), P("chan"), P()),
        out_specs=(P("day", "chan", None), P("day", None)),
        check_vma=False,
    )
```

time: 175 us -> 43 us (0.25)
  waiting for transfers between devices: 96.2 us -> 0 us
  Pallas kernels: 0 us -> 35.4 us
  blocking collectives: 32.7 us -> 0 us
  other arithmetic: 23.3 us -> 0 us
  between operations: 14.1 us -> 0.65 us
  matrix products: 2.9 us -> 0 us
    psum x2 -> x0, waiting for transfers between devices: 96.2 us -> none  [the longest x1 72.4 us: per_device(): summed = lax.psum(picked.astype(jnp.bfloat16), 'chan')]
    pallas_call x0 -> x1, Pallas kernels: none -> 35.4 us  [per_device(): pl.pallas_call(functools.partial(kernel, n, days), out_shape=(jax.ShapeDt...]
    psum x1 -> x0, blocking collectives: 32.7 us -> none  [per_device(): lax.psum((jnp.stack(numers, 0), jnp.stack(denoms, 0)), 'chan')]
    another operation x2 -> x0, other arithmetic: 19.4 us -> none
    unnamed x9, local copies, waits for them, and re-layouts: 2.18 us -> 5.4 us
    dot_general x2 -> x0, matrix products: 2.9 us -> none  [the longest x1 1.97 us: correlate_block(): jnp.dot(cross, table, preferred_element_type=jnp.float32)]
    reduce_sum x2 -> x0, other arithmetic: 2.2 us -> none  [the longest x1 2.05 us: per_device(): den_chan = jnp.sum(weighted * slope, axis=(0, 2))]
    slice x2 -> x0, local copies, waits for them, and re-layouts: 2.12 us -> none  [the longest x1 1.57 us: correlate_block(): real_src = chosen[:, None, 0]]
  transfers between devices with their start and end apart: 2 -> 0, of which waited for: 2 -> 0; matrix products, arithmetic and copies ran while one was open for 12% -> 0% of each run, Pallas kernels for 0% -> 0%
where the time goes in v1:
time: 43 us; the launch traced here: 42.7 us
  Pallas kernels  35.4 us (82%)
  local copies, waits for them, and re-layouts  6.67 us (16%)
  between operations  0.65 us (2%)
    pallas_call x1, Pallas kernels, per_device(): pl.pallas_call(functools.partial(kernel, n, days), out_shape=(jax.ShapeDt...  35.4 us
    unnamed x9, local copies, waits for them, and re-layouts  5.4 us
    another operation x2, local copies, waits for them, and re-layouts, per_device(): local = spectra[0].reshape(ch, 2, n, chunk).transpose(2, 1, 0, 3)  1.27 us

profile of v1, /device:TPU:0, one launch (start us, length us, event | category | flops | bytes accessed | tf_op | source)
XLA Modules:
  0.0 42.7 jit_solution(16546883106830575860)
XLA Ops:
  0.6 1.1 %reshape.4 = bf16[16,2,16,256]{3,2,1,0:T(8,128)(2,1)S(1)} reshape(bf16[1,16,2,4096]{3,2,1,0:T(2,128)(2,1)} %param.5) | data formatting | bytes 524288 | tf_op jit(solution)/shard_map/reshape;squeeze | solution.py:212
  1.8 0.2 copy.14
  1.9 0.8 %copy.10.bounds_ref = s32[16,2]{1,0:T(8,128)S(1)} copy(s32[16,2]{0,1:T(2,128)} %param.8) | data formatting | bytes 256 | tf_op args[3]
  2.7 0.0 copy-start
  2.7 2.2 %copy-done = bf16[16,512,256]{2,1,0:T(8,128)(2,1)S(1)} copy-done((bf16[16,512,256]{2,1,0:T(8,128)(2,1)S(1)}, bf16[16,512,256]{2,1,0:T(8,128)(2,1)}, u32[]{:S(2)}) %copy-start) | copy-done | bytes 4194328
  4.9 0.0 copy-start.1
  4.9 0.7 %copy-done.1 = s32[16]{0:T(128)S(1)} copy-done((s32[16]{0:T(128)S(1)}, s32[16]{0:T(128)}, u32[]{:S(2)}) %copy-start.1) | copy-done | bytes 88
  5.5 0.0 copy-start.2
  5.5 0.7 %copy-done.2 = s32[16]{0:T(128)S(1)} copy-done((s32[16]{0:T(128)S(1)}, s32[16]{0:T(128)}, u32[]{:S(2)}) %copy-start.2) | copy-done | bytes 88
  6.2 35.4 %shard_map.68 = (bf16[8,16,256]{2,1,0:T(8,128)(2,1)S(1)}, f32[1,8]{1,0:T(1,128)S(1)}) custom-call(s32[16,2]{1,0:T(8,128)S(1)} %copy.10.bounds_ref, s32[1,16]{1,0:T(1,128)S(1)} %bitcast.6, s32[1,16]{1,0:T(1,128)S(1)} %bitcast.7, bf16[16,2,16,256]{3,2,1,0:T(8,128)(2,1)S(1)} %bitcast.5, bf16[16,512,256]{2,1,0:T(8,128)(2,1)S(1)} %copy-done), custom_call_target="tpu_custom_call" | custom-call | tf_op jit(solution)/shard_map/pallas_call | solution.py:216
  41.6 0.6 %copy.17 = bf16[8,16,256]{2,1,0:T(8,128)(2,1)} copy(bf16[8,16,256]{2,1,0:T(8,128)(2,1)S(1)} %get-tuple-element.4) | data formatting | bytes 131072
  42.2 0.5 %copy.18 = f32[1,8]{1,0:T(1,128)} copy(f32[1,8]{1,0:T(1,128)S(1)} %get-tuple-element.5) | data formatting | bytes 64
Async XLA Ops:
  2.7 2.2 %copy-start = (bf16[16,512,256]{2,1,0:T(8,128)(2,1)S(1)}, bf16[16,512,256]{2,1,0:T(8,128)(2,1)}, u32[]{:S(2)}) copy-start(bf16[16,512,256]{2,1,0:T(8,128)(2,1)} %constant.2.clone.table_hbm) | copy-start | bytes 12582916
  4.9 0.7 %copy-start.1 = (s32[16]{0:T(128)S(1)}, s32[16]{0:T(128)}, u32[]{:S(2)}) copy-start(s32[16]{0:T(128)} %param.6) | copy-start | bytes 196
  5.5 0.7 %copy-start.2 = (s32[16]{0:T(128)S(1)}, s32[16]{0:T(128)}, u32[]{:S(2)}) copy-start(s32[16]{0:T(128)} %param.7) | copy-start | bytes 196

commit v2 on v1

v2 whole, which is shorter than its diff:
```python
import functools
import math

import jax
import jax.numpy as jnp
import numpy as np
from jax import lax
from jax.experimental import pallas as pl
from jax.experimental.pallas import tpu as pltpu
from jax.sharding import PartitionSpec as P

LAGS = 256
NINT = 8
LANES = 128
MESH = pl.DeviceIdType.MESH


def lag_table(bins, lags):
    freq = np.arange(bins, dtype=np.int32)
    shift = np.arange(lags, dtype=np.int32) - lags // 2
    phase = freq[:, None] * shift[None, :] % (2 * bins)
    angle = np.float32(math.pi) * phase.astype(np.float32) / np.float32(bins)
    scale = np.float32(1.0 / math.sqrt(bins))
    return np.stack([np.cos(angle) * scale, -np.sin(angle) * scale]).astype(jnp.bfloat16)


def column(row):
    m = row.shape[1]
    wide = jnp.broadcast_to(row.astype(jnp.float32), (m, m))
    eye = lax.broadcasted_iota(jnp.int32, (m, m), 0) == lax.broadcasted_iota(jnp.int32, (m, m), 1)
    return jnp.sum(jnp.where(eye, wide, 0.0), axis=1, keepdims=True)


def kernel(
    outers, inners, days, bounds_hbm, index_hbm, inter_hbm, local_hbm, table_hbm, ref_out, drift_out,
    bounds_ref, index_ref, inter_ref, local_ref, window, table, mine, parts, half, parts2, gath, cross, acc, day_send, day_recv, fit,
    in_sem, table_sem, rs_send, rs_recv, rt_send, rt_recv, ag_send, ag_recv, fw_send, fw_recv,
    dy_send, dy_recv, fp_send, fp_recv, ft_send, ft_recv,
):
    n = outers * inners
    me = lax.axis_index("chan")
    outer, inner = me // inners, lax.rem(me, inners)
    today = lax.axis_index("day")
    ch = local_ref.shape[2]
    nsrc = mine.shape[3]
    chunk = mine.shape[4]
    share = nsrc // days
    rows = share * ch

    load = pltpu.make_async_copy(table_hbm, table, table_sem)
    ins = [
        pltpu.make_async_copy(src, dst, in_sem.at[i])
        for i, (src, dst) in enumerate([
            (index_hbm, index_ref), (local_hbm, local_ref),
            (inter_hbm, inter_ref), (bounds_hbm, bounds_ref),
        ])
    ]
    for copy in ins:
        copy.start()
    load.start()

    barrier = pltpu.get_barrier_semaphore()

    def along(o, i, d):
        chan = lax.rem(outer + o, outers) * inners + lax.rem(inner + i, inners)
        return {"chan": chan, "day": lax.rem(today + d, days)}

    partners = [(o, 0, 0) for o in range(1, outers)]
    partners += [(0, i, d) for d in range(days) for i in range(inners) if i or d]
    for partner in partners:
        pl.semaphore_signal(barrier, inc=1, device_id=along(*partner), device_id_type=MESH)

    for copy in ins:
        copy.wait()

    wanted = column(index_ref[...]) - (me * ch).astype(jnp.float32)
    select = (
        wanted == lax.broadcasted_iota(jnp.int32, (nsrc, ch), 1).astype(jnp.float32)
    ).astype(jnp.bfloat16)

    for i in range(inners):
        for o in range(outers):
            for part in range(2):
                mine[i, o, part] = jnp.dot(
                    select, local_ref[o * inners + i, part], preferred_element_type=jnp.float32
                ).astype(jnp.bfloat16)
    pl.semaphore_wait(barrier, len(partners))

    def remote(src, dst, send_sem, recv_sem, to):
        return pltpu.make_async_remote_copy(
            src_ref=src, dst_ref=dst, send_sem=send_sem, recv_sem=recv_sem,
            device_id=along(*to), device_id_type=MESH,
        )

    scatter = [
        remote(mine.at[lax.rem(inner + i, inners)], parts.at[i], rs_send.at[i], rs_recv.at[i], (0, i, 0))
        for i in range(1, inners)
    ]
    across = [
        remote(half.at[lax.rem(outer + o, outers)], parts2.at[o], rt_send.at[o], rt_recv.at[o], (o, 0, 0))
        for o in range(1, outers)
    ]
    gather = [
        remote(gath.at[0, 0], gath.at[0, o], ag_send.at[o], ag_recv.at[o], (o, 0, 0))
        for o in range(1, outers)
    ]
    forward = [
        [
            remote(gath.at[0, o], gath.at[i, o], fw_send.at[i, o], fw_recv.at[i, o], (0, i, 0))
            for i in range(1, inners)
        ]
        for o in range(outers)
    ]
    for copy in scatter:
        copy.start()
    some = mine[inner].astype(jnp.float32)
    for i, copy in enumerate(scatter):
        copy.wait_recv()
        some = some + parts[i + 1].astype(jnp.float32)
    half[...] = some.astype(jnp.bfloat16)
    for copy in across:
        copy.start()
    own = half[outer].astype(jnp.float32)
    for o, copy in enumerate(across):
        copy.wait_recv()
        own = own + parts2[o + 1].astype(jnp.float32)
    gath[0, 0] = own.astype(jnp.bfloat16)
    for copy in gather + forward[0]:
        copy.start()
    load.wait()

    def correlate(i, o):
        j = lax.rem(outer - o + outers, outers) * inners + lax.rem(inner - i + inners, inners)
        sr = local_ref[j, 0].astype(jnp.float32)
        si = local_ref[j, 1].astype(jnp.float32)
        vr = gath[i, o, 0].astype(jnp.float32)
        vi = gath[i, o, 1].astype(jnp.float32)
        for s in range(nsrc):
            ar, ai = vr[s : s + 1], vi[s : s + 1]
            at = pl.ds(s * ch, ch)
            cross[at, :chunk] = (sr * ar + si * ai).astype(jnp.bfloat16)
            cross[at, chunk:] = (si * ar - sr * ai).astype(jnp.bfloat16)
        return jnp.dot(cross[...], table[j], preferred_element_type=jnp.float32)

    bounds = bounds_ref[...]
    at = lax.broadcasted_iota(jnp.int32, (nsrc, LAGS), 1).astype(jnp.float32)
    window[...] = (
        (at >= column(bounds[0:1])) & (at < column(bounds[1:2]))
    ).astype(jnp.float32)
    acc[...] = correlate(0, 0)
    for o in range(1, outers):
        gather[o - 1].wait_recv()
        for copy in forward[o]:
            copy.start()
    for o in range(1, outers):
        acc[...] += correlate(0, o)

    def step(o, carry):
        for i in range(1, inners):
            remote(
                gath.at[0, o], gath.at[i, o], fw_send.at[i, o], fw_recv.at[i, o], (0, i, 0)
            ).wait_recv()
            acc[...] += correlate(i, o)
        return carry

    lax.fori_loop(0, outers, step, 0)

    exchange = [
        remote(
            day_send.at[lax.rem(today + k, days)], day_recv.at[k], dy_send.at[k], dy_recv.at[k], (0, 0, k)
        )
        for k in range(1, days)
    ]
    for d in range(days):
        day_send[d] = acc[d * rows : (d + 1) * rows].astype(jnp.bfloat16)
    for copy in exchange:
        copy.start()

    lag = lax.broadcasted_iota(jnp.int32, (ch, LAGS), 1)
    member = (
        column(inter_ref[...]) == lax.broadcasted_iota(jnp.int32, (ch, LANES), 1).astype(jnp.float32)
    ).astype(jnp.float32)
    late = (
        column(inter_ref[...]) + LANES // 2
        == lax.broadcasted_iota(jnp.int32, (ch, LANES), 1).astype(jnp.float32)
    ).astype(jnp.float32)
    base = today * rows
    for copy in exchange:
        copy.wait_recv()
    nums = [jnp.zeros((ch, LAGS), jnp.float32) for _ in range(days)]
    dens = [jnp.zeros((ch, LAGS), jnp.float32) for _ in range(days)]
    for s in range(share):
        corrs = [acc[pl.ds(pl.multiple_of(base + s * ch, ch), ch)]]
        for k in range(1, days):
            corrs.append(day_recv[k, s * ch : (s + 1) * ch].astype(jnp.float32))
        mean = (sum(corrs[1:], corrs[0]) / days).astype(jnp.bfloat16)
        ref_out[s] = mean
        mean = mean.astype(jnp.float32)
        inside = window[pl.ds(today * share + s, 1)]
        for k in range(days):
            after = jnp.where(lag == LAGS - 1, 0.0, pltpu.roll(corrs[k], LAGS - 1, 1))
            before = jnp.where(lag == 0, 0.0, pltpu.roll(corrs[k], 1, 1))
            slope = 0.5 * (after - before)
            weighted = slope * inside
            nums[k] = nums[k] + weighted * (corrs[k] - mean)
            dens[k] = dens[k] + weighted * slope
    for k in range(days):
        num = jnp.sum(nums[k], axis=1, keepdims=True)
        den = jnp.sum(dens[k], axis=1, keepdims=True)
        fit[(days - k) % days] = jnp.sum(num * member + den * late, axis=0, keepdims=True)

    def landing(i, d):
        return days + d * inners + i

    plane = [
        remote(fit.at[d], fit.at[landing(i, d)], fp_send.at[i, d], fp_recv.at[i, d], (0, i, d))
        for d in range(days) for i in range(inners) if i or d
    ]
    for copy in plane:
        copy.start()
    total = fit[0]
    for copy in plane:
        copy.wait_recv()
    for d in range(days):
        for i in range(inners):
            if i or d:
                total = total + fit[landing(i, d)]
    held = days + days * inners
    fit[held] = total
    final = [
        remote(fit.at[held], fit.at[held + o], ft_send.at[o], ft_recv.at[o], (o, 0, 0))
        for o in range(1, outers)
    ]
    for copy in final:
        copy.start()
    for o, copy in enumerate(final):
        copy.wait_recv()
        total = total + fit[held + o + 1]
    drift_out[...] = (total / (pltpu.roll(total, LANES // 2, 1) + 1e-06))[:, :NINT]

    for copy in scatter + across + gather + sum(forward, []) + exchange + plane + final:
        copy.wait_send()


def per_device(n, days, spectra, source_index, interrogator, lag_bounds):
    _, ch, _, bins = spectra.shape
    nsrc = source_index.shape[0]
    chunk = bins // n
    share = nsrc // days
    inners = math.gcd(n, 4)
    outers = n // inners
    table = lag_table(bins, LAGS).reshape(2, n, chunk, LAGS).transpose(1, 0, 2, 3)
    table = jnp.asarray(table.reshape(n, 2 * chunk, LAGS))
    local = spectra[0].reshape(ch, 2, n, chunk).transpose(2, 1, 0, 3)
    vmem = pl.BlockSpec(memory_space=pltpu.VMEM)
    dma = pltpu.SemaphoreType.DMA
    bf16, f32 = jnp.bfloat16, jnp.float32
    ref_out, drift = pl.pallas_call(
        functools.partial(kernel, outers, inners, days),
        out_shape=(
            jax.ShapeDtypeStruct((share, ch, LAGS), bf16),
            jax.ShapeDtypeStruct((1, NINT), f32),
        ),
        in_specs=[
            pl.BlockSpec(memory_space=pl.ANY) for _ in range(5)
        ],
        out_specs=(vmem, vmem),
        scratch_shapes=[
            pltpu.VMEM((2, nsrc), jnp.int32),
            pltpu.VMEM((1, nsrc), jnp.int32),
            pltpu.VMEM((1, ch), jnp.int32),
            pltpu.VMEM((n, 2, ch, chunk), bf16),
            pltpu.VMEM((nsrc, LAGS), f32),
            pltpu.VMEM((n, 2 * chunk, LAGS), bf16),
            pltpu.VMEM((inners, outers, 2, nsrc, chunk), bf16),
            pltpu.VMEM((inners, outers, 2, nsrc, chunk), bf16),
            pltpu.VMEM((outers, 2, nsrc, chunk), bf16),
            pltpu.VMEM((outers, 2, nsrc, chunk), bf16),
            pltpu.VMEM((inners, outers, 2, nsrc, chunk), bf16),
            pltpu.VMEM((nsrc * ch, 2 * chunk), bf16),
            pltpu.VMEM((nsrc * ch, LAGS), f32),
            pltpu.VMEM((days, share * ch, LAGS), bf16),
            pltpu.VMEM((days, share * ch, LAGS), bf16),
            pltpu.VMEM((days + days * inners + outers, 1, LANES), f32),
            dma((4,)), dma, dma((inners,)), dma((inners,)), dma((outers,)), dma((outers,)),
            dma((outers,)), dma((outers,)), dma((inners, outers)), dma((inners, outers)),
            dma((days,)), dma((days,)), dma((inners, days)), dma((inners, days)),
            dma((outers,)), dma((outers,)),
        ],
        compiler_params=pltpu.CompilerParams(
            collective_id=0, has_side_effects=True, vmem_limit_bytes=60 * 1024 * 1024
        ),
    )(lag_bounds.T, source_index[None], interrogator[None], local, table)
    return ref_out, drift


def solution(mesh):
    return jax.shard_map(
        functools.partial(per_device, mesh.shape["chan"], mesh.shape["day"]),
        mesh=mesh,
        in_specs=(P("day", "chan", None, None), P(), P("chan"), P()),
        out_specs=(P("day", "chan", None), P("day", None)),
        check_vma=False,
    )
```

time: 43 us -> 37.4 us (0.87)
  Pallas kernels: 35.4 us -> 32 us
  local copies, waits for them, and re-layouts: 6.67 us -> 4.55 us
    pallas_call x1, Pallas kernels: 35.4 us -> 32 us  [per_device(): pl.pallas_call(functools.partial(kernel, outers, inners, days), out_shape...]
    unnamed x9 -> x2, local copies, waits for them, and re-layouts: 5.4 us -> 2.59 us
    another operation x2, local copies, waits for them, and re-layouts: 1.27 us -> 1.96 us  [per_device(): local = spectra[0].reshape(ch, 2, n, chunk).transpose(2, 1, 0, 3)]
where the time goes in v2:
time: 37.4 us; the launch traced here: 37.2 us
  Pallas kernels  32 us (86%)
  local copies, waits for them, and re-layouts  4.55 us (12%)
  between operations  0.64 us (2%)
    pallas_call x1, Pallas kernels, per_device(): pl.pallas_call(functools.partial(kernel, outers, inners, days), out_shape...  32 us
    unnamed x2, local copies, waits for them, and re-layouts  2.59 us
    another operation x2, local copies, waits for them, and re-layouts, per_device(): local = spectra[0].reshape(ch, 2, n, chunk).transpose(2, 1, 0, 3)  1.96 us

profile of v2, /device:TPU:0, one launch (start us, length us, event | category | flops | bytes accessed | tf_op | source)
XLA Modules:
  0.0 37.2 jit_solution(8550882957172035506)
XLA Ops:
  0.6 1.1 %reshape.4 = bf16[16,2,16,256]{3,2,1,0:T(8,128)(2,1)S(1)} reshape(bf16[1,16,2,4096]{3,2,1,0:T(2,128)(2,1)} %param.5) | data formatting | bytes 524288 | tf_op jit(solution)/shard_map/reshape;squeeze | solution.py:254
  1.8 0.8 %copy.12 = bf16[16,2,16,256]{3,0,1,2:T(8,128)(2,1)} copy(bf16[16,2,16,256]{3,2,1,0:T(8,128)(2,1)S(1)} %reshape.4) | data formatting | bytes 524288 | tf_op jit(solution)/shard_map/reshape;squeeze | solution.py:254
  2.6 32.0 %shard_map.68 = (bf16[8,16,256]{2,1,0:T(8,128)(2,1)}, f32[1,8]{1,0:T(1,128)}) custom-call(s32[2,16]{1,0:T(2,128)} %bitcast.7, s32[1,16]{1,0:T(1,128)} %bitcast.8, s32[1,16]{1,0:T(1,128)} %bitcast.9, bf16[16,2,16,256]{3,2,1,0:T(8,128)(2,1)} %bitcast.6, bf16[16,512,256]{2,1,0:T(8,128)(2,1)} %constant.2.clone.table_hbm), custom_call_target="tpu_custom_call" | custom-call | tf_op jit(solution)/shard_map/pallas_call | solution.py:258
  34.6 1.5 %copy.15 = bf16[8,16,256]{2,1,0:T(8,128)(2,1)} copy(bf16[8,16,256]{2,1,0:T(8,128)(2,1)} %get-tuple-element.4) | data formatting | bytes 131072
  36.1 1.1 %copy.16 = f32[1,8]{1,0:T(1,128)} copy(f32[1,8]{1,0:T(1,128)} %get-tuple-element.5) | data formatting | bytes 64

commit v3 on v2

--- a/solution.py
+++ b/solution.py
@@ -33,8 +33,8 @@
 
 def kernel(
     outers, inners, days, bounds_hbm, index_hbm, inter_hbm, local_hbm, table_hbm, ref_out, drift_out,
-    bounds_ref, index_ref, inter_ref, local_ref, window, table, mine, parts, half, parts2, gath, cross, acc, day_send, day_recv, fit,
-    in_sem, table_sem, rs_send, rs_recv, rt_send, rt_recv, ag_send, ag_recv, fw_send, fw_recv,
+    bounds_ref, index_ref, inter_ref, local_ref, window, table, mine, parts, gath, cross, acc, day_send, day_recv, fit,
+    in_sem, table_sem, rs_send, rs_recv, ag_send, ag_recv, fw_send, fw_recv,
     dy_send, dy_recv, fp_send, fp_recv, ft_send, ft_recv,
 ):
     n = outers * inners
@@ -65,8 +65,9 @@
         chan = lax.rem(outer + o, outers) * inners + lax.rem(inner + i, inners)
         return {"chan": chan, "day": lax.rem(today + d, days)}
 
-    partners = [(o, 0, 0) for o in range(1, outers)]
-    partners += [(0, i, d) for d in range(days) for i in range(inners) if i or d]
+    others = [(o, i) for o in reversed(range(outers)) for i in range(inners) if o or i]
+    partners = [(o, i, 0) for o, i in others]
+    partners += [(0, i, d) for d in range(1, days) for i in range(inners)]
     for partner in partners:
         pl.semaphore_signal(barrier, inc=1, device_id=along(*partner), device_id_type=MESH)
 
@@ -93,12 +94,11 @@
         )
 
     scatter = [
-        remote(mine.at[lax.rem(inner + i, inners)], parts.at[i], rs_send.at[i], rs_recv.at[i], (0, i, 0))
-        for i in range(1, inners)
-    ]
-    across = [
-        remote(half.at[lax.rem(outer + o, outers)], parts2.at[o], rt_send.at[o], rt_recv.at[o], (o, 0, 0))
-        for o in range(1, outers)
+        remote(
+            mine.at[lax.rem(inner + i, inners), lax.rem(outer + o, outers)], parts.at[i, o],
+            rs_send.at[i, o], rs_recv.at[i, o], (o, i, 0),
+        )
+        for o, i in others
     ]
     gather = [
         remote(gath.at[0, 0], gath.at[0, o], ag_send.at[o], ag_recv.at[o], (o, 0, 0))
@@ -113,17 +113,10 @@
     ]
     for copy in scatter:
         copy.start()
-    some = mine[inner].astype(jnp.float32)
-    for i, copy in enumerate(scatter):
-        copy.wait_recv()
-        some = some + parts[i + 1].astype(jnp.float32)
-    half[...] = some.astype(jnp.bfloat16)
-    for copy in across:
-        copy.start()
-    own = half[outer].astype(jnp.float32)
-    for o, copy in enumerate(across):
-        copy.wait_recv()
-        own = own + parts2[o + 1].astype(jnp.float32)
+    own = mine[inner, outer].astype(jnp.float32)
+    for (o, i), copy in zip(others, scatter):
+        copy.wait_recv()
+        own = own + parts[i, o].astype(jnp.float32)
     gath[0, 0] = own.astype(jnp.bfloat16)
     for copy in gather + forward[0]:
         copy.start()
@@ -238,7 +231,7 @@
         total = total + fit[held + o + 1]
     drift_out[...] = (total / (pltpu.roll(total, LANES // 2, 1) + 1e-06))[:, :NINT]
 
-    for copy in scatter + across + gather + sum(forward, []) + exchange + plane + final:
+    for copy in scatter + gather + sum(forward, []) + exchange + plane + final:
         copy.wait_send()
 
 
@@ -274,15 +267,13 @@
             pltpu.VMEM((n, 2 * chunk, LAGS), bf16),
             pltpu.VMEM((inners, outers, 2, nsrc, chunk), bf16),
             pltpu.VMEM((inners, outers, 2, nsrc, chunk), bf16),
-            pltpu.VMEM((outers, 2, nsrc, chunk), bf16),
-            pltpu.VMEM((outers, 2, nsrc, chunk), bf16),
             pltpu.VMEM((inners, outers, 2, nsrc, chunk), bf16),
             pltpu.VMEM((nsrc * ch, 2 * chunk), bf16),
             pltpu.VMEM((nsrc * ch, LAGS), f32),
             pltpu.VMEM((days, share * ch, LAGS), bf16),
             pltpu.VMEM((days, share * ch, LAGS), bf16),
             pltpu.VMEM((days + days * inners + outers, 1, LANES), f32),
-            dma((4,)), dma, dma((inners,)), dma((inners,)), dma((outers,)), dma((outers,)),
+            dma((4,)), dma, dma((inners, outers)), dma((inners, outers)),
             dma((outers,)), dma((outers,)), dma((inners, outers)), dma((inners, outers)),
             dma((days,)), dma((days,)), dma((inners, days)), dma((inners, days)),
             dma((outers,)), dma((outers,)),

time: 37.4 us -> 37.8 us (1.011)
  Pallas kernels: 32 us -> 32.4 us
    pallas_call x1, Pallas kernels: 32 us -> 32.4 us  [per_device(): pl.pallas_call(functools.partial(kernel, outers, inners, days), out_shape...]
where the time goes in v3:
time: 37.8 us; the launch traced here: 37.6 us
  Pallas kernels  32.4 us (86%)
  local copies, waits for them, and re-layouts  4.55 us (12%)
  between operations  0.64 us (2%)
    pallas_call x1, Pallas kernels, per_device(): pl.pallas_call(functools.partial(kernel, outers, inners, days), out_shape...  32.4 us
    unnamed x2, local copies, waits for them, and re-layouts  2.59 us
    another operation x2, local copies, waits for them, and re-layouts, per_device(): local = spectra[0].reshape(ch, 2, n, chunk).transpose(2, 1, 0, 3)  1.96 us

profile of v3, /device:TPU:0, one launch (start us, length us, event | category | flops | bytes accessed | tf_op | source)
XLA Modules:
  0.0 37.6 jit_solution(8682828481350623619)
XLA Ops:
  0.6 1.1 %reshape.4 = bf16[16,2,16,256]{3,2,1,0:T(8,128)(2,1)S(1)} reshape(bf16[1,16,2,4096]{3,2,1,0:T(2,128)(2,1)} %param.5) | data formatting | bytes 524288 | tf_op jit(solution)/shard_map/reshape;squeeze | solution.py:247
  1.8 0.8 %copy.12 = bf16[16,2,16,256]{3,0,1,2:T(8,128)(2,1)} copy(bf16[16,2,16,256]{3,2,1,0:T(8,128)(2,1)S(1)} %reshape.4) | data formatting | bytes 524288 | tf_op jit(solution)/shard_map/reshape;squeeze | solution.py:247
  2.6 32.4 %shard_map.68 = (bf16[8,16,256]{2,1,0:T(8,128)(2,1)}, f32[1,8]{1,0:T(1,128)}) custom-call(s32[2,16]{1,0:T(2,128)} %bitcast.7, s32[1,16]{1,0:T(1,128)} %bitcast.8, s32[1,16]{1,0:T(1,128)} %bitcast.9, bf16[16,2,16,256]{3,2,1,0:T(8,128)(2,1)} %bitcast.6, bf16[16,512,256]{2,1,0:T(8,128)(2,1)} %constant.2.clone.table_hbm), custom_call_target="tpu_custom_call" | custom-call | tf_op jit(solution)/shard_map/pallas_call | solution.py:251
  35.0 1.5 %copy.15 = bf16[8,16,256]{2,1,0:T(8,128)(2,1)} copy(bf16[8,16,256]{2,1,0:T(8,128)(2,1)} %get-tuple-element.4) | data formatting | bytes 131072
  36.5 1.1 %copy.16 = f32[1,8]{1,0:T(1,128)} copy(f32[1,8]{1,0:T(1,128)} %get-tuple-element.5) | data formatting | bytes 64
